TPU v7x, 128 devices: a whole 4x4x4 slice. The times are simulated.
128 devices in a mesh: gx: 16 (over z, y), gy: 8 (over x, core).
Axes of the slice: x: 4, y: 4, z: 4, core: 2. Of those that a mesh axis runs over, the one named last changes fastest.
Arguments:
- pressure: float32 [128, 1024, 128], P('gx', 'gy'), may hold values from 0.5 to 1.5
- water_sat: float32 [128, 1024, 128], P('gx', 'gy'), may hold values from 0.1 to 0.45
- gas_sat: float32 [128, 1024, 128], P('gx', 'gy'), may hold values from 0 to 0.4
- mass_old: float32 [3, 128, 1024, 128], P(None, 'gx', 'gy'), may hold values from 0.1 to 0.7
- pore_volume: float32 [128, 1024, 128], P('gx', 'gy'), may hold values from 0.5 to 2
- permeability: float32 [128, 1024, 128], P('gx', 'gy'), may hold values from 0.1 to 10
- newton_scale: float32 [3, 128, 1024, 128], P(None, 'gx', 'gy'), may hold values from 0.1 to 0.4
- conn_factor: float32 [49152, 128], P(('gx', 'gy')), may hold values from 0.2 to 2
- perf_column: int32 [49152], P(('gx', 'gy')), may hold values from 0 to 1023
- perf_owner: int32 [49152, 1], P(('gx', 'gy')), may hold values from 0 to 127; in each aligned block of 384 rows (0 to 383, 384 to 767, ...) at most 6 rows name the same one
- perf_well: int32 [49152], P(('gx', 'gy')), may hold values from 0 to 7
- perf_segment: int32 [49152], P(('gx', 'gy')), may hold values from 0 to 7
- seg_parent: int32 [1024, 8], P(('gx', 'gy')), may hold values from 0 to 6, as said below
- seg_drop: float32 [1024, 8], P(('gx', 'gy')), may hold values from 0.1 to 0.5
- bottom_press: float32 [1024], P(('gx', 'gy')), may hold values from 0.2 to 0.6
Outputs:
- residual: float32 [3, 128, 1024, 128], P(None, 'gx', 'gy')
- seg_pressure: float32 [1024, 8], P(('gx', 'gy'))
Inputs may be any that keep to these rules, and one draw needn't show every extreme that they name: `perf_owner`: in the rows of one device at most 6 name the same owner, a bound that some block reaches; every device owns wells with perforations. `seg_parent`: segment 0 of a well is its own parent; the parent of a segment s >= 1 is a segment below s.
All inputs are finite; a program needn't handle non-finite values.
Results may differ from a plain program's by a relative error of at most 0.0003.
Values sent between devices are 32-bit elements; how exact they have to be, the bound alone decides.
A program may use at most 128 MiB of HBM per device.

v0:
```python
import functools

import jax
import jax.numpy as jnp
from jax import lax
from jax.experimental import pallas as pl
from jax.experimental.pallas import tpu as pltpu
from jax.sharding import PartitionSpec as P

MESH = pl.DeviceIdType.MESH
F32 = jnp.float32
BF16 = jnp.bfloat16
NGX, NGY = 16, 8
CX, CY, NZ = 8, 128, 128
PD = 384
COLS = CX * CY
YB = 32


def split(v):
    hi = v.astype(BF16)
    return hi, (v - hi.astype(F32)).astype(BF16)


def dot2(one_hot, v):
    hi, lo = split(v)
    return jnp.dot(one_hot, hi, preferred_element_type=F32) + jnp.dot(
        one_hot, lo, preferred_element_type=F32
    )


def exact_dot(a, b, dims=(((1,), (0,)), ((), ()))):
    return lax.dot_general(a, b, dims, precision=lax.Precision.HIGHEST, preferred_element_type=F32)


def mobilities(p, sw, sg):
    so = 1.0 - sw - sg
    m1 = (0.5 * so * so) * (0.95 + 0.05 * p)
    m2 = (2.0 * sw * sw) * (0.98 + 0.02 * p)
    m3 = (5.0 * sg * sg) * (0.2 + 0.8 * p)
    m4 = m1 * (0.2 * p)
    return m1, m2, m3, m4


def total_mobility(sw, sg):
    so = 1.0 - sw - sg
    return 0.5 * so * so + 2.0 * sw * sw + 5.0 * sg * sg


def side_flux(p_i, m_i, p_j, m_j, trans):
    d = p_i - p_j
    up = d > 0.0
    t = trans * d
    return [t * jnp.where(up, a, b) for a, b in zip(m_i, m_j)]


def harmonic(a, b):
    return 2.0 * a * b / (a + b)


def kernel(
    p_h, sw_h, sg_h, mo_h, pv_h, k_h, ns_h, cf_h,
    col_ref, own_ref, well_ref, seg_ref, par_ref, drop_ref, bot_ref,
    out_ref, press_ref,
    st1, st2, cf, pv, mo, ns, hx1, hx2, hy1, hy2, hys1, hys2,
    q, tx, ty, tz, txb, tyb, fx, fy, base, c0, wl,
    g, s, a_t, r, lm, mlh, mll,
    tb, r1, x1, r2, x3, r3, w0, wr,
    load_sem, halo_send, halo_recv, ph_send, ph_recv, w_send, w_recv,
):
    gx = lax.axis_index("gx")
    gy = lax.axis_index("gy")

    barrier = pltpu.get_barrier_semaphore()
    for k in range(1, NGX):
        pl.semaphore_signal(barrier, 1, device_id=(lax.rem(gx + k, NGX), gy), device_id_type=MESH)
    for k in range(1, NGY):
        pl.semaphore_signal(barrier, 1, device_id=(gx, lax.rem(gy + k, NGY)), device_id_type=MESH)

    loads = [
        pltpu.make_async_copy(p_h, st1.at[0], load_sem.at[0]),
        pltpu.make_async_copy(sw_h, st1.at[1], load_sem.at[1]),
        pltpu.make_async_copy(sg_h, st1.at[2], load_sem.at[2]),
        pltpu.make_async_copy(cf_h, cf, load_sem.at[3]),
        pltpu.make_async_copy(k_h, st1.at[3], load_sem.at[4]),
        pltpu.make_async_copy(pv_h, pv, load_sem.at[5]),
        pltpu.make_async_copy(mo_h, mo, load_sem.at[6]),
        pltpu.make_async_copy(ns_h, ns, load_sem.at[7]),
    ]
    for load in loads:
        load.start()

    col = col_ref[...]
    own = own_ref[...]
    row = lax.rem(own, NGY) * 8 + seg_ref[...]
    lane = (own // NGY) * 8 + well_ref[...]
    packed = (col + 1024 * row + 65536 * lane).astype(F32)
    packed_t = jnp.transpose(jnp.broadcast_to(packed, (128, PD))).astype(jnp.int32)
    col_t = packed_t & 1023
    row_t = (packed_t >> 10) & 63
    lane_t = packed_t >> 16
    lanes = lax.broadcasted_iota(jnp.int32, (PD, 128), 1)
    lm[...] = jnp.where(lane_t == lanes, 1.0, 0.0)
    r[...] = jnp.where(row_t == lanes, 1.0, 0.0).astype(BF16)
    for j in range(CX):
        g[:, j * 128 : (j + 1) * 128] = jnp.where(col_t == lanes + 128 * j, 1.0, 0.0).astype(BF16)
    rows64 = lax.broadcasted_iota(jnp.int32, (64, PD), 0)
    a_t[...] = jnp.where(row == rows64, 1.0, 0.0).astype(BF16)

    def prep(x, state):
        p, sw, sg = state[0, x], state[1, x], state[2, x]
        m1, m2, m3, m4 = mobilities(p, sw, sg)
        q[0, x, 0:CY] = p
        q[1, x, 0:CY] = m1
        q[2, x, 0:CY] = m2
        q[3, x, 0:CY] = m3 + m4
        here = pl.ds(pl.multiple_of(x * CY, CY), CY)
        mixed = 0.8 * m1 + m2 + 0.15 * m3
        hi, lo = split(mixed)
        mlh[here, 0:128] = hi
        mll[here, 0:128] = lo
        hi, lo = split(total_mobility(sw, sg))
        mlh[here, 128:256] = hi
        mll[here, 128:256] = lo

    def well_sums(n):
        seen = jnp.dot(g[...], mlh[...], preferred_element_type=F32) + jnp.dot(
            g[...], mll[...], preferred_element_type=F32
        )
        num = jnp.sum(cf[...] * seen[:, 0:128], axis=1, keepdims=True)
        den = jnp.sum(cf[...] * seen[:, 128:256], axis=1, keepdims=True)
        spread = jnp.concatenate([lm[...] * num, lm[...] * den], axis=1)
        tb[n] = dot2(a_t[...], spread)

    def wait_bytes(ref, sem):
        pltpu.make_async_copy(ref, ref, sem).wait()

    def send_one(n):
        for k in (4, 3, 5, 2, 6, 1, 7):
            to = lax.rem(gy + k, NGY)
            pltpu.make_async_remote_copy(
                tb.at[n, pl.ds(pl.multiple_of(to * 8, 8), 8)], r1.at[n, k - 1],
                ph_send.at[n, 0], ph_recv.at[n, 0], device_id=(gx, to), device_id_type=MESH,
            ).start()

    def send_two(n):
        wait_bytes(r1.at[n], ph_recv.at[n, 0])
        x1[n] = tb[n, pl.ds(pl.multiple_of(gy * 8, 8), 8)] + jnp.sum(r1[n], axis=0)
        for k in (10, 9, 11, 6, 14, 2, 8, 5, 7, 13, 15, 1, 3, 4, 12):
            to = lax.rem(gx + k, NGX)
            pltpu.make_async_remote_copy(
                x1.at[n], r2.at[n, k - 1],
                ph_send.at[n, 1], ph_recv.at[n, 1], device_id=(to, gy), device_id_type=MESH,
            ).start()

    def send_three(n):
        wait_bytes(r2.at[n], ph_recv.at[n, 1])
        sums = x1[n] + jnp.sum(r2[n], axis=0)
        if n == 0:
            wait_bytes(wr, w_recv)
            w0[...] = w0[...] + jnp.sum(wr[...], axis=0)
        drop = w0[0:8]
        parent = w0[8:16]
        dens = (sums[:, 0:128] + 0.5) / (sums[:, 128:256] + 1.0)
        rise = dens * drop
        seg = lax.broadcasted_iota(jnp.int32, (8, 128), 0)
        press = jnp.where(seg == 0, parent + rise, rise)
        for above in range(7):
            hit = (seg > above) & (parent == float(above))
            press = press + jnp.where(hit, press[above : above + 1], 0.0)
        answer = jnp.concatenate([press, dens], axis=1)
        x3[n] = answer
        mine = pl.ds(pl.multiple_of(gy * 8, 8), 8)
        r3[n, mine] = answer
        for k in (4, 3, 5, 2, 6, 1, 7):
            to = lax.rem(gy + k, NGY)
            pltpu.make_async_remote_copy(
                x3.at[n], r3.at[n, mine],
                ph_send.at[n, 2], ph_recv.at[n, 2], device_id=(gx, to), device_id_type=MESH,
            ).start()
        return press

    def answers(n):
        wait_bytes(r3.at[n, pl.ds(0, 56)], ph_recv.at[n, 2])
        seen = dot2(r[:, 0:64], r3[n])
        press = jnp.sum(lm[...] * seen[:, 0:128], axis=1, keepdims=True)
        dens = jnp.sum(lm[...] * seen[:, 128:256], axis=1, keepdims=True)
        depth = (lax.broadcasted_iota(jnp.int32, (1, NZ), 1).astype(F32) + 0.5) / NZ - 0.5
        wl[...] = dot2(s[...], cf[...] * (press + (0.5 * dens) * depth))

    def pack_rows(state, rows, fields):
        for f in range(fields):
            for x in range(CX):
                rows[0, f, x : x + 1] = state[f, x, CY - 1 : CY]
                rows[1, f, x : x + 1] = state[f, x, 0:1]

    def halo_copies(n, state, planes, rows_out, rows_in, fields):
        up, down = lax.rem(gx + 1, NGX), lax.rem(gx + NGX - 1, NGX)
        right, left = lax.rem(gy + 1, NGY), lax.rem(gy + NGY - 1, NGY)
        four = (
            (state.at[pl.ds(0, fields), CX - 1], planes.at[0], (up, gy)),
            (state.at[pl.ds(0, fields), 0], planes.at[1], (down, gy)),
            (rows_out.at[0], rows_in.at[0], (gx, right)),
            (rows_out.at[1], rows_in.at[1], (gx, left)),
        )
        return [
            pltpu.make_async_remote_copy(
                src, dst, halo_send.at[n, i], halo_recv.at[n, i], device_id=to, device_id_type=MESH
            )
            for i, (src, dst, to) in enumerate(four)
        ]

    def inner_faces(x, c):
        for y0 in range(0, CY, YB):
            ys = slice(y0, y0 + YB)
            p, m1, m2, m34 = (q[f, x, ys] for f in range(4))
            n = [q[f, x + 1, ys] for f in range(4)]
            flow = side_flux(p, (m1, m2, m34), n[0], n[1:], tx[x, ys])
            acc = []
            for f in range(3):
                acc.append(flow[f] - fx[f, ys])
                fx[f, ys] = flow[f]
            n = [q[f, x, y0 + 1 : y0 + 1 + YB] for f in range(4)]
            flow = side_flux(p, (m1, m2, m34), n[0], n[1:], ty[x, ys])
            for f in range(3):
                fy[f, 8 + y0 : 8 + y0 + YB] = flow[f]
                acc[f] = acc[f] + (flow[f] - fy[f, 7 + y0 : 7 + y0 + YB])
            m4 = m1 * (0.2 * p)
            m3 = m34 - m4
            pn, n1, n2, n3, n4 = (pltpu.roll(v, NZ - 1, 1) for v in (p, m1, m2, m3, m4))
            d, total = p - pn, p + pn
            phi1 = d + (0.001 * total + 0.038)
            phi2 = d + (0.0005 * total + 0.049)
            phi3 = d + (0.003 * total + 0.0015)
            t = tz[x, ys]
            up1 = phi1 > 0.0
            t1 = t * phi1
            flow = (
                t1 * jnp.where(up1, m1, n1),
                (t * phi2) * jnp.where(phi2 > 0.0, m2, n2),
                (t * phi3) * jnp.where(phi3 > 0.0, m3, n3) + t1 * jnp.where(up1, m4, n4),
            )
            for f in range(3):
                acc[f] = acc[f] + (flow[f] - pltpu.roll(flow[f], 1, 1))
            sw, sg = c[1, x, ys], c[2, x, ys]
            stored1 = (0.95 + 0.05 * p) * (1.0 - sw - sg)
            stored2 = (0.98 + 0.02 * p) * sw
            stored3 = (0.2 + 0.8 * p) * sg + (0.2 * p) * stored1
            vol = pv[x, ys]
            for f, held in enumerate((stored1, stored2, stored3)):
                base[f, x, ys] = vol * held - mo[f, x, ys] + acc[f]

    def plane_faces(planes):
        for side, x in ((0, 0), (1, CX - 1)):
            ph = planes[side, 0]
            h1, h2, h3, h4 = mobilities(ph, planes[side, 1], planes[side, 2])
            there, here = (h1, h2, h3 + h4), [q[f, x, 0:CY] for f in (1, 2, 3)]
            p = q[0, x, 0:CY]
            if side == 0:
                flow = side_flux(ph, there, p, here, txb[0])
            else:
                flow = side_flux(p, here, ph, there, txb[1])
            for f in range(3):
                base[f, x] = base[f, x] - flow[f] if side == 0 else base[f, x] + flow[f]

    def row_faces(rows, rows_out):
        for side, y in ((0, 0), (1, CY - 1)):
            ph = rows[side, 0]
            h1, h2, h3, h4 = mobilities(ph, rows[side, 1], rows[side, 2])
            own_side = 1 - side
            p = rows_out[own_side, 0]
            m1, m2, m3, m4 = mobilities(p, rows_out[own_side, 1], rows_out[own_side, 2])
            there, here = (h1, h2, h3 + h4), (m1, m2, m3 + m4)
            if side == 0:
                flow = side_flux(ph, there, p, here, tyb[0])
            else:
                flow = side_flux(p, here, ph, there, tyb[1])
            for f in range(3):
                change = -flow[f] if side == 0 else flow[f]
                for x in range(CX):
                    base[f, x, y : y + 1] = base[f, x, y : y + 1] + change[x : x + 1]

    def transmissibility(x, c):
        k = st1[3, x]
        nxt = st1[3, jnp.minimum(x + 1, CX - 1)]
        tx[x] = harmonic(k, nxt) * jnp.where(x < CX - 1, 1.0, 0.0)
        ys = lax.broadcasted_iota(jnp.int32, (CY, NZ), 0)
        zs = lax.broadcasted_iota(jnp.int32, (CY, NZ), 1)
        ty[x] = jnp.where(ys == CY - 1, 0.0, harmonic(k, pltpu.roll(k, CY - 1, 0)))
        tz[x] = jnp.where(zs == NZ - 1, 0.0, 0.1 * harmonic(k, pltpu.roll(k, NZ - 1, 1)))
        return c

    def each_plane(body):
        def step(x, c):
            body(x)
            return c
        lax.fori_loop(0, CX, step, 0)

    for i in range(3):
        loads[i].wait()
    each_plane(lambda x: prep(x, st1))
    loads[3].wait()
    well_sums(0)
    pl.semaphore_wait(barrier, NGX - 1 + NGY - 1)
    send_one(0)

    eye = jnp.where(
        lax.broadcasted_iota(jnp.int32, (8, 8), 0) == lax.broadcasted_iota(jnp.int32, (8, 8), 1), 1.0, 0.0
    )
    place = jnp.where(
        lax.broadcasted_iota(jnp.int32, (8, 128), 0) + gx * 8 == lax.broadcasted_iota(jnp.int32, (8, 128), 1),
        1.0, 0.0,
    )
    flip = (((1,), (1,)), ((), ()))
    w0[0:8] = exact_dot(exact_dot(eye, drop_ref[...], flip), place)
    w0[8:16] = exact_dot(exact_dot(eye, par_ref[...].astype(F32), flip), place)
    w0[8:9] = exact_dot(bot_ref[...], place)
    w_copies = []
    for k in range(1, NGX):
        w_copies.append(pltpu.make_async_remote_copy(
            w0, wr.at[k - 1], w_send, w_recv,
            device_id=(lax.rem(gx + k, NGX), gy), device_id_type=MESH,
        ))
    for copy in w_copies:
        copy.start()

    loads[4].wait()
    pack_rows(st1, hys1, 4)
    halo_one = halo_copies(0, st1, hx1, hys1, hy1, 4)
    for copy in halo_one:
        copy.start()

    for f in range(4):
        q[f, CX] = jnp.zeros((CY + 8, NZ), F32)
        for x in range(CX):
            q[f, x, CY : CY + 8] = jnp.zeros((8, NZ), F32)
    for f in range(3):
        fx[f] = jnp.zeros((CY, NZ), F32)
        fy[f, 0:8] = jnp.zeros((8, NZ), F32)
    each_row = lax.broadcasted_iota(jnp.int32, (128, PD), 0)
    for j in range(CX):
        s[j * 128 : (j + 1) * 128] = jnp.where(col == each_row + 128 * j, 1.0, 0.0).astype(BF16)
    c0[...] = dot2(s[...], cf[...])
    for i in range(5, 8):
        loads[i].wait()
    wait_bytes(wr, w_send)
    send_two(0)
    lax.fori_loop(0, CX, transmissibility, 0)
    each_plane(lambda x: inner_faces(x, st1))
    send_three(0)
    for copy in halo_one:
        copy.wait()
    for side, x, there in ((0, 0, gx > 0), (1, CX - 1, gx < NGX - 1)):
        txb[side] = harmonic(hx1[side, 3], st1[3, x]) * jnp.where(there, 1.0, 0.0)
    for side, there in ((0, gy > 0), (1, gy < NGY - 1)):
        tyb[side] = harmonic(hy1[side, 3], hys1[1 - side, 3]) * jnp.where(there, 1.0, 0.0)
    plane_faces(hx1)
    row_faces(hy1, hys1)
    answers(0)

    def update(x):
        here = pl.ds(pl.multiple_of(x * CY, CY), CY)
        drive = q[0, x, 0:CY] * c0[here] - wl[here]
        for f in range(3):
            first = base[f, x] + q[f + 1, x, 0:CY] * drive
            st2[f, x] = st1[f, x] - ns[f, x] * first
        prep(x, st2)

    each_plane(update)
    well_sums(1)
    send_one(1)
    pack_rows(st2, hys2, 3)
    halo_two = halo_copies(1, st2, hx2, hys2, hy2, 3)
    for copy in halo_two:
        copy.start()
    for f in range(3):
        fx[f] = jnp.zeros((CY, NZ), F32)
    send_two(1)
    each_plane(lambda x: inner_faces(x, st2))
    press = send_three(1)
    press_ref[...] = exact_dot(place, press, flip)
    for copy in halo_two:
        copy.wait()
    plane_faces(hx2)
    row_faces(hy2, hys2)
    answers(1)

    def finish(x):
        here = pl.ds(pl.multiple_of(x * CY, CY), CY)
        drive = q[0, x, 0:CY] * c0[here] - wl[here]
        for f in range(3):
            out_ref[f, x] = base[f, x] + q[f + 1, x, 0:CY] * drive

    each_plane(finish)
    for n in range(2):
        wait_bytes(r1.at[n], ph_send.at[n, 0])
        wait_bytes(r2.at[n], ph_send.at[n, 1])
        wait_bytes(r3.at[n, pl.ds(0, 56)], ph_send.at[n, 2])


def shards(
    pressure, water_sat, gas_sat, mass_old, pore_volume, permeability, newton_scale, conn_factor,
    perf_column, perf_owner, perf_well, perf_segment, seg_parent, seg_drop, bottom_press,
):
    vmem = pl.BlockSpec(memory_space=pltpu.VMEM)
    hbm = pl.BlockSpec(memory_space=pl.ANY)
    cells = (CX, CY, NZ)
    dma = pltpu.SemaphoreType.DMA
    scratch = [
        pltpu.VMEM((4,) + cells, F32),
        pltpu.VMEM((3,) + cells, F32),
        pltpu.VMEM((PD, NZ), F32),
        pltpu.VMEM(cells, F32),
        pltpu.VMEM((3,) + cells, F32),
        pltpu.VMEM((3,) + cells, F32),
        pltpu.VMEM((2, 4, CY, NZ), F32),
        pltpu.VMEM((2, 3, CY, NZ), F32),
        pltpu.VMEM((2, 4, CX, NZ), F32),
        pltpu.VMEM((2, 3, CX, NZ), F32),
        pltpu.VMEM((2, 4, CX, NZ), F32),
        pltpu.VMEM((2, 3, CX, NZ), F32),
        pltpu.VMEM((4, CX + 1, CY + 8, NZ), F32),
        pltpu.VMEM(cells, F32),
        pltpu.VMEM(cells, F32),
        pltpu.VMEM(cells, F32),
        pltpu.VMEM((2, CY, NZ), F32),
        pltpu.VMEM((2, CX, NZ), F32),
        pltpu.VMEM((3, CY, NZ), F32),
        pltpu.VMEM((3, CY + 8, NZ), F32),
        pltpu.VMEM((3,) + cells, F32),
        pltpu.VMEM((COLS, NZ), F32),
        pltpu.VMEM((COLS, NZ), F32),
        pltpu.VMEM((PD, COLS), BF16),
        pltpu.VMEM((COLS, PD), BF16),
        pltpu.VMEM((64, PD), BF16),
        pltpu.VMEM((PD, 128), BF16),
        pltpu.VMEM((PD, 128), F32),
        pltpu.VMEM((COLS, 256), BF16),
        pltpu.VMEM((COLS, 256), BF16),
        pltpu.VMEM((2, 64, 256), F32),
        pltpu.VMEM((2, NGY - 1, 8, 256), F32),
        pltpu.VMEM((2, 8, 256), F32),
        pltpu.VMEM((2, NGX - 1, 8, 256), F32),
        pltpu.VMEM((2, 8, 256), F32),
        pltpu.VMEM((2, 64, 256), F32),
        pltpu.VMEM((16, 128), F32),
        pltpu.VMEM((NGX - 1, 16, 128), F32),
        dma((8,)), dma((2, 4)), dma((2, 4)), dma((2, 3)), dma((2, 3)), dma, dma,
    ]
    return pl.pallas_call(
        kernel,
        out_shape=(
            jax.ShapeDtypeStruct((3,) + cells, F32),
            jax.ShapeDtypeStruct((8, 8), F32),
        ),
        in_specs=[hbm] * 8 + [vmem] * 7,
        out_specs=(vmem, vmem),
        scratch_shapes=scratch,
        compiler_params=pltpu.CompilerParams(
            collective_id=0, has_side_effects=True, vmem_limit_bytes=48 << 20
        ),
    )(
        pressure, water_sat, gas_sat, mass_old, pore_volume, permeability, newton_scale, conn_factor,
        perf_column.reshape(1, PD), perf_owner.reshape(1, PD), perf_well.reshape(1, PD),
        perf_segment.reshape(1, PD), seg_parent, seg_drop, bottom_press.reshape(1, 8),
    )


def solution(mesh):
    cell = P("gx", "gy", None)
    triple = P(None, "gx", "gy", None)
    flat = P(("gx", "gy"))
    rows = P(("gx", "gy"), None)
    return jax.shard_map(
        shards,
        mesh=mesh,
        in_specs=(
            cell, cell, cell, triple, cell, cell, triple,
            rows, flat, rows, flat, flat, rows, rows, flat,
        ),
        out_specs=(triple, rows),
        check_vma=False,
    )
```

profile of v0, /device:TPU:1, one launch (start us, length us, event | category | flops | bytes accessed | tf_op | source)
XLA Modules:
  0.0 56.6 jit_solution(9684888616460465121)
XLA Ops:
  0.6 0.7 %reshape.19.col_ref = s32[1,384]{1,0:T(1,128)S(1)} reshape(s32[384]{0:T(512)} %param.23) | data formatting | bytes 3072 | tf_op jit(solution)/shard_map/reshape | solution.py:464
  1.3 0.7 %reshape.21.well_ref = s32[1,384]{1,0:T(1,128)S(1)} reshape(s32[384]{0:T(512)} %param.25) | data formatting | bytes 3072 | tf_op jit(solution)/shard_map/reshape | solution.py:464
  2.0 0.7 %reshape.22.seg_ref = s32[1,384]{1,0:T(1,128)S(1)} reshape(s32[384]{0:T(512)} %param.26) | data formatting | bytes 3072 | tf_op jit(solution)/shard_map/reshape | solution.py:465
  2.7 0.0 copy-start
  2.7 1.4 %copy-done = f32[3,8,128,128]{3,2,1,0:T(8,128)S(1)} copy-done((f32[3,8,128,128]{3,2,1,0:T(8,128)S(1)}, f32[3,8,128,128]{3,2,1,0:T(8,128)}, u32[]{:S(2)}) %copy-start) | copy-done | bytes 1572888
  4.1 0.0 copy-start.1
  4.1 1.0 %copy-done.1 = f32[8,128,128]{2,1,0:T(8,128)S(1)} copy-done((f32[8,128,128]{2,1,0:T(8,128)S(1)}, f32[8,128,128]{2,1,0:T(8,128)}, u32[]{:S(2)}) %copy-start.1) | copy-done | bytes 524312
  5.1 0.0 copy-start.2
  5.1 1.0 %copy-done.2 = f32[8,128,128]{2,1,0:T(8,128)S(1)} copy-done((f32[8,128,128]{2,1,0:T(8,128)S(1)}, f32[8,128,128]{2,1,0:T(8,128)}, u32[]{:S(2)}) %copy-start.2) | copy-done | bytes 524312
  6.2 0.0 copy-start.3
  6.2 1.0 %copy-done.3 = f32[8,128,128]{2,1,0:T(8,128)S(1)} copy-done((f32[8,128,128]{2,1,0:T(8,128)S(1)}, f32[8,128,128]{2,1,0:T(8,128)}, u32[]{:S(2)}) %copy-start.3) | copy-done | bytes 524312
  7.2 1.0 %copy-done.4 = f32[8,128,128]{2,1,0:T(8,128)S(1)} copy-done((f32[8,128,128]{2,1,0:T(8,128)S(1)}, f32[8,128,128]{2,1,0:T(8,128)}, u32[]{:S(2)}) %copy-start.4) | copy-done | bytes 524312
  8.3 0.0 copy-start.5
  8.3 1.0 %copy-done.5 = f32[8,128,128]{2,1,0:T(8,128)S(1)} copy-done((f32[8,128,128]{2,1,0:T(8,128)S(1)}, f32[8,128,128]{2,1,0:T(8,128)}, u32[]{:S(2)}) %copy-start.5) | copy-done | bytes 524312
  9.3 0.0 copy-start.6
  9.3 0.9 %copy-done.6 = f32[384,128]{1,0:T(8,128)S(1)} copy-done((f32[384,128]{1,0:T(8,128)S(1)}, f32[384,128]{1,0:T(8,128)}, u32[]{:S(2)}) %copy-start.6) | copy-done | bytes 196632
  10.2 0.0 copy-start.7
  10.2 0.7 %copy-done.7 = s32[8,8]{1,0:T(8,128)S(1)} copy-done((s32[8,8]{1,0:T(8,128)S(1)}, s32[8,8]{1,0:T(8,128)}, u32[]{:S(2)}) %copy-start.7) | copy-done | bytes 280
  10.9 0.7 %copy-done.8 = f32[8,8]{1,0:T(8,128)S(1)} copy-done((f32[8,8]{1,0:T(8,128)S(1)}, f32[8,8]{1,0:T(8,128)}, u32[]{:S(2)}) %copy-start.8) | copy-done | bytes 280
  11.6 0.7 %copy-done.9 = s32[384,1]{0,1:T(1,128)S(1)} copy-done((s32[384,1]{0,1:T(1,128)S(1)}, s32[384,1]{0,1:T(1,128)}, u32[]{:S(2)}) %copy-start.9) | copy-done | bytes 1560
  12.3 0.7 %copy-done.10 = f32[8]{0:T(128)S(1)} copy-done((f32[8]{0:T(128)S(1)}, f32[8]{0:T(128)}, u32[]{:S(2)}) %copy-start.10) | copy-done | bytes 56
  12.9 41.9 %shard_map.158 = (f32[3,8,128,128]{3,2,1,0:T(8,128)S(1)}, f32[8,8]{1,0:T(8,128)S(1)}) custom-call(f32[8,128,128]{2,1,0:T(8,128)S(1)} %copy-done.1, f32[8,128,128]{2,1,0:T(8,128)S(1)} %copy-done.2, f32[8,128,128]{2,1,0:T(8,128)S(1)} %copy-done.3, f32[3,8,128,128]{3,2,1,0:T(8,128)S(1)} %copy-done, f32[8,128,128]{2,1,0:T(8,128)S(1)} %copy-done.4, ...), custom_call_target="tpu_custom_call" | custom-call | tf_op jit(solution)/shard_map/pallas_call | solution.py:450
  54.8 1.1 %copy.19 = f32[3,8,128,128]{3,2,1,0:T(8,128)} copy(f32[3,8,128,128]{3,2,1,0:T(8,128)S(1)} %get-tuple-element.4) | data formatting | bytes 3145728
  56.0 0.6 %copy.20 = f32[8,8]{1,0:T(8,128)} copy(f32[8,8]{1,0:T(8,128)S(1)} %get-tuple-element.5) | data formatting | bytes 512
  (4 shorter events, 0.0 us)
Async XLA Ops:
  2.7 1.4 %copy-start = (f32[3,8,128,128]{3,2,1,0:T(8,128)S(1)}, f32[3,8,128,128]{3,2,1,0:T(8,128)}, u32[]{:S(2)}) copy-start(f32[3,8,128,128]{3,2,1,0:T(8,128)} %mo_h.1) | copy-start | bytes 4718596
  4.1 1.0 %copy-start.1 = (f32[8,128,128]{2,1,0:T(8,128)S(1)}, f32[8,128,128]{2,1,0:T(8,128)}, u32[]{:S(2)}) copy-start(f32[8,128,128]{2,1,0:T(8,128)} %p_h.1) | copy-start | bytes 1572868
  5.1 1.0 %copy-start.2 = (f32[8,128,128]{2,1,0:T(8,128)S(1)}, f32[8,128,128]{2,1,0:T(8,128)}, u32[]{:S(2)}) copy-start(f32[8,128,128]{2,1,0:T(8,128)} %sw_h.1) | copy-start | bytes 1572868
  6.2 1.0 %copy-start.3 = (f32[8,128,128]{2,1,0:T(8,128)S(1)}, f32[8,128,128]{2,1,0:T(8,128)}, u32[]{:S(2)}) copy-start(f32[8,128,128]{2,1,0:T(8,128)} %sg_h.1) | copy-start | bytes 1572868
  7.2 1.0 %copy-start.4 = (f32[8,128,128]{2,1,0:T(8,128)S(1)}, f32[8,128,128]{2,1,0:T(8,128)}, u32[]{:S(2)}) copy-start(f32[8,128,128]{2,1,0:T(8,128)} %pv_h.1) | copy-start | bytes 1572868
  8.3 1.0 %copy-start.5 = (f32[8,128,128]{2,1,0:T(8,128)S(1)}, f32[8,128,128]{2,1,0:T(8,128)}, u32[]{:S(2)}) copy-start(f32[8,128,128]{2,1,0:T(8,128)} %k_h.1) | copy-start | bytes 1572868
  9.3 0.9 %copy-start.6 = (f32[384,128]{1,0:T(8,128)S(1)}, f32[384,128]{1,0:T(8,128)}, u32[]{:S(2)}) copy-start(f32[384,128]{1,0:T(8,128)} %cf_h.1) | copy-start | bytes 589828
  10.2 0.7 %copy-start.7 = (s32[8,8]{1,0:T(8,128)S(1)}, s32[8,8]{1,0:T(8,128)}, u32[]{:S(2)}) copy-start(s32[8,8]{1,0:T(8,128)} %par_ref.1) | copy-start | bytes 772
  10.9 0.7 %copy-start.8 = (f32[8,8]{1,0:T(8,128)S(1)}, f32[8,8]{1,0:T(8,128)}, u32[]{:S(2)}) copy-start(f32[8,8]{1,0:T(8,128)} %drop_ref.1) | copy-start | bytes 772
  11.6 0.7 %copy-start.9 = (s32[384,1]{0,1:T(1,128)S(1)}, s32[384,1]{0,1:T(1,128)}, u32[]{:S(2)}) copy-start(s32[384,1]{0,1:T(1,128)} %param.24) | copy-start | bytes 4612
  12.3 0.7 %copy-start.10 = (f32[8]{0:T(128)S(1)}, f32[8]{0:T(128)}, u32[]{:S(2)}) copy-start(f32[8]{0:T(128)} %param.29) | copy-start | bytes 100
where the time goes:
time: 57.1 us; the launch traced here: 56.6 us
  Pallas kernels  41.9 us (73%)
  local copies, waits for them, and re-layouts  14 us (25%)
  between operations  0.65 us (1%)
    pallas_call x1, Pallas kernels, shards(): pl.pallas_call(kernel, out_shape=(jax.ShapeDtypeStruct((3,) + cells, F32)...  41.9 us
    unnamed x24, local copies, waits for them, and re-layouts  12 us

commit v1 on v0

--- a/solution.py
+++ b/solution.py
@@ -15,6 +15,8 @@
 PD = 384
 COLS = CX * CY
 YB = 32
+GX_ORDER = (10, 9, 11, 6, 14, 2, 8, 5, 7, 13, 15, 1, 3, 4, 12)
+GY_ORDER = (4, 3, 5, 2, 6, 1, 7)
 
 
 def split(v):
@@ -60,23 +62,27 @@
 
 def kernel(
     p_h, sw_h, sg_h, mo_h, pv_h, k_h, ns_h, cf_h,
-    col_ref, own_ref, well_ref, seg_ref, par_ref, drop_ref, bot_ref,
+    col_h, own_h, well_h, seg_h, par_h, drop_h, bot_h,
     out_ref, press_ref,
     st1, st2, cf, pv, mo, ns, hx1, hx2, hy1, hy2, hys1, hys2,
-    q, tx, ty, tz, txb, tyb, fx, fy, base, c0, wl,
-    g, s, a_t, r, lm, mlh, mll,
-    tb, r1, x1, r2, x3, r3, w0, wr,
-    load_sem, halo_send, halo_recv, ph_send, ph_recv, w_send, w_recv,
+    hk, q, tx, ty, tz, txb, tyb, fx, fy, base, c0, wl,
+    g, s, a_t, r, lm, mlh, mll, same, ct, edge, dh, dl, gq, eh, el, vhl,
+    tb, r1, x1, r2, y1, r4, x3, r3, wd,
+    col_ref, own_ref, well_ref, seg_ref, par_ref, drop_ref, bot_ref,
+    small_sem, load_sem, halo_send, halo_recv, k_send, k_recv, ph_send, ph_recv,
 ):
     gx = lax.axis_index("gx")
     gy = lax.axis_index("gy")
 
-    barrier = pltpu.get_barrier_semaphore()
-    for k in range(1, NGX):
-        pl.semaphore_signal(barrier, 1, device_id=(lax.rem(gx + k, NGX), gy), device_id_type=MESH)
-    for k in range(1, NGY):
-        pl.semaphore_signal(barrier, 1, device_id=(gx, lax.rem(gy + k, NGY)), device_id_type=MESH)
-
+    small = [
+        pltpu.make_async_copy(src, dst, small_sem.at[i])
+        for i, (src, dst) in enumerate((
+            (col_h, col_ref), (own_h, own_ref), (well_h, well_ref), (seg_h, seg_ref),
+            (par_h, par_ref), (drop_h, drop_ref), (bot_h, bot_ref),
+        ))
+    ]
+    for load in small:
+        load.start()
     loads = [
         pltpu.make_async_copy(p_h, st1.at[0], load_sem.at[0]),
         pltpu.make_async_copy(sw_h, st1.at[1], load_sem.at[1]),
@@ -87,19 +93,28 @@
         pltpu.make_async_copy(mo_h, mo, load_sem.at[6]),
         pltpu.make_async_copy(ns_h, ns, load_sem.at[7]),
     ]
-    for load in loads:
+    for load in loads[:4]:
         load.start()
 
-    col = col_ref[...]
+    barrier = pltpu.get_barrier_semaphore()
+    for k in GX_ORDER:
+        pl.semaphore_signal(barrier, 1, device_id=(lax.rem(gx + k, NGX), gy), device_id_type=MESH)
+    for k in GY_ORDER:
+        pl.semaphore_signal(barrier, 1, device_id=(gx, lax.rem(gy + k, NGY)), device_id_type=MESH)
+
+    for load in small:
+        load.wait()
+    col = col_ref[...].reshape(1, PD)
     own = own_ref[...]
-    row = lax.rem(own, NGY) * 8 + seg_ref[...]
-    lane = (own // NGY) * 8 + well_ref[...]
+    row = lax.rem(own, NGY) * 8 + seg_ref[...].reshape(1, PD)
+    lane = (own // NGY) * 8 + well_ref[...].reshape(1, PD)
     packed = (col + 1024 * row + 65536 * lane).astype(F32)
     packed_t = jnp.transpose(jnp.broadcast_to(packed, (128, PD))).astype(jnp.int32)
     col_t = packed_t & 1023
     row_t = (packed_t >> 10) & 63
     lane_t = packed_t >> 16
     lanes = lax.broadcasted_iota(jnp.int32, (PD, 128), 1)
+    ct[...] = col_t
     lm[...] = jnp.where(lane_t == lanes, 1.0, 0.0)
     r[...] = jnp.where(row_t == lanes, 1.0, 0.0).astype(BF16)
     for j in range(CX):
@@ -107,13 +122,15 @@
     rows64 = lax.broadcasted_iota(jnp.int32, (64, PD), 0)
     a_t[...] = jnp.where(row == rows64, 1.0, 0.0).astype(BF16)
 
-    def prep(x, state):
+    def prep(x, state, sums):
         p, sw, sg = state[0, x], state[1, x], state[2, x]
         m1, m2, m3, m4 = mobilities(p, sw, sg)
         q[0, x, 0:CY] = p
         q[1, x, 0:CY] = m1
         q[2, x, 0:CY] = m2
         q[3, x, 0:CY] = m3 + m4
+        if not sums:
+            return
         here = pl.ds(pl.multiple_of(x * CY, CY), CY)
         mixed = 0.8 * m1 + m2 + 0.15 * m3
         hi, lo = split(mixed)
@@ -123,20 +140,20 @@
         mlh[here, 128:256] = hi
         mll[here, 128:256] = lo
 
-    def well_sums(n):
-        seen = jnp.dot(g[...], mlh[...], preferred_element_type=F32) + jnp.dot(
-            g[...], mll[...], preferred_element_type=F32
-        )
-        num = jnp.sum(cf[...] * seen[:, 0:128], axis=1, keepdims=True)
-        den = jnp.sum(cf[...] * seen[:, 128:256], axis=1, keepdims=True)
+    def well_sums(n, mixed, total):
+        num = jnp.sum(cf[...] * mixed, axis=1, keepdims=True)
+        den = jnp.sum(cf[...] * total, axis=1, keepdims=True)
         spread = jnp.concatenate([lm[...] * num, lm[...] * den], axis=1)
         tb[n] = dot2(a_t[...], spread)
 
     def wait_bytes(ref, sem):
         pltpu.make_async_copy(ref, ref, sem).wait()
 
+    out_parts = (x1, y1)
+    in_parts = (r2, r4)
+
     def send_one(n):
-        for k in (4, 3, 5, 2, 6, 1, 7):
+        for k in GY_ORDER:
             to = lax.rem(gy + k, NGY)
             pltpu.make_async_remote_copy(
                 tb.at[n, pl.ds(pl.multiple_of(to * 8, 8), 8)], r1.at[n, k - 1],
@@ -145,22 +162,25 @@
 
     def send_two(n):
         wait_bytes(r1.at[n], ph_recv.at[n, 0])
-        x1[n] = tb[n, pl.ds(pl.multiple_of(gy * 8, 8), 8)] + jnp.sum(r1[n], axis=0)
-        for k in (10, 9, 11, 6, 14, 2, 8, 5, 7, 13, 15, 1, 3, 4, 12):
+        part = tb[n, pl.ds(pl.multiple_of(gy * 8, 8), 8)] + jnp.sum(r1[n], axis=0)
+        if n == 0:
+            x1[:, 0:256] = part
+        else:
+            y1[...] = part
+        for k in GX_ORDER:
             to = lax.rem(gx + k, NGX)
             pltpu.make_async_remote_copy(
-                x1.at[n], r2.at[n, k - 1],
+                out_parts[n], in_parts[n].at[k - 1],
                 ph_send.at[n, 1], ph_recv.at[n, 1], device_id=(to, gy), device_id_type=MESH,
             ).start()
 
     def send_three(n):
-        wait_bytes(r2.at[n], ph_recv.at[n, 1])
-        sums = x1[n] + jnp.sum(r2[n], axis=0)
+        wait_bytes(in_parts[n], ph_recv.at[n, 1])
+        sums = out_parts[n][...] + jnp.sum(in_parts[n][...], axis=0)
         if n == 0:
-            wait_bytes(wr, w_recv)
-            w0[...] = w0[...] + jnp.sum(wr[...], axis=0)
-        drop = w0[0:8]
-        parent = w0[8:16]
+            wd[...] = sums[:, 256:512]
+        drop = wd[:, 0:128]
+        parent = wd[:, 128:256]
         dens = (sums[:, 0:128] + 0.5) / (sums[:, 128:256] + 1.0)
         rise = dens * drop
         seg = lax.broadcasted_iota(jnp.int32, (8, 128), 0)
@@ -172,7 +192,7 @@
         x3[n] = answer
         mine = pl.ds(pl.multiple_of(gy * 8, 8), 8)
         r3[n, mine] = answer
-        for k in (4, 3, 5, 2, 6, 1, 7):
+        for k in GY_ORDER:
             to = lax.rem(gy + k, NGY)
             pltpu.make_async_remote_copy(
                 x3.at[n], r3.at[n, mine],
@@ -186,7 +206,13 @@
         press = jnp.sum(lm[...] * seen[:, 0:128], axis=1, keepdims=True)
         dens = jnp.sum(lm[...] * seen[:, 128:256], axis=1, keepdims=True)
         depth = (lax.broadcasted_iota(jnp.int32, (1, NZ), 1).astype(F32) + 0.5) / NZ - 0.5
-        wl[...] = dot2(s[...], cf[...] * (press + (0.5 * dens) * depth))
+        hi, lo = split(cf[...] * (press + (0.5 * dens) * depth))
+        vhl[:, 0:128] = hi
+        vhl[:, 128:256] = lo
+
+    def spread_answers():
+        both = jnp.dot(s[...], vhl[...], preferred_element_type=F32)
+        wl[...] = both[:, 0:128] + both[:, 128:256]
 
     def pack_rows(state, rows, fields):
         for f in range(fields):
@@ -194,12 +220,12 @@
                 rows[0, f, x : x + 1] = state[f, x, CY - 1 : CY]
                 rows[1, f, x : x + 1] = state[f, x, 0:1]
 
-    def halo_copies(n, state, planes, rows_out, rows_in, fields):
+    def halo_copies(n, state, planes, rows_out, rows_in):
         up, down = lax.rem(gx + 1, NGX), lax.rem(gx + NGX - 1, NGX)
         right, left = lax.rem(gy + 1, NGY), lax.rem(gy + NGY - 1, NGY)
         four = (
-            (state.at[pl.ds(0, fields), CX - 1], planes.at[0], (up, gy)),
-            (state.at[pl.ds(0, fields), 0], planes.at[1], (down, gy)),
+            (state.at[pl.ds(0, 3), CX - 1], planes.at[0], (up, gy)),
+            (state.at[pl.ds(0, 3), 0], planes.at[1], (down, gy)),
             (rows_out.at[0], rows_in.at[0], (gx, right)),
             (rows_out.at[1], rows_in.at[1], (gx, left)),
         )
@@ -250,7 +276,12 @@
             for f, held in enumerate((stored1, stored2, stored3)):
                 base[f, x, ys] = vol * held - mo[f, x, ys] + acc[f]
 
-    def plane_faces(planes):
+    def put_edge(start, size, f, change):
+        hi, lo = split(change)
+        eh[start : start + size, f * 128 : (f + 1) * 128] = hi
+        el[start : start + size, f * 128 : (f + 1) * 128] = lo
+
+    def plane_faces(planes, edges):
         for side, x in ((0, 0), (1, CX - 1)):
             ph = planes[side, 0]
             h1, h2, h3, h4 = mobilities(ph, planes[side, 1], planes[side, 2])
@@ -262,8 +293,12 @@
                 flow = side_flux(p, here, ph, there, txb[1])
             for f in range(3):
                 base[f, x] = base[f, x] - flow[f] if side == 0 else base[f, x] + flow[f]
-
-    def row_faces(rows, rows_out):
+                if edges:
+                    change = ns[f, x] * flow[f] if side == 0 else -ns[f, x] * flow[f]
+                    put_edge(side * CY, CY, f, change)
+
+    def row_faces(rows, rows_out, edges):
+        row_edges = []
         for side, y in ((0, 0), (1, CY - 1)):
             ph = rows[side, 0]
             h1, h2, h3, h4 = mobilities(ph, rows[side, 1], rows[side, 2])
@@ -279,6 +314,12 @@
                 change = -flow[f] if side == 0 else flow[f]
                 for x in range(CX):
                     base[f, x, y : y + 1] = base[f, x, y : y + 1] + change[x : x + 1]
+                if edges:
+                    scale = jnp.concatenate([ns[f, x, y : y + 1] for x in range(CX)], axis=0)
+                    row_edges.append((f, -scale * change))
+        if edges:
+            for f in range(3):
+                put_edge(2 * CY, 16, f, jnp.concatenate([v for i, v in row_edges if i == f], axis=0))
 
     def transmissibility(x, c):
         k = st1[3, x]
@@ -296,40 +337,57 @@
             return c
         lax.fori_loop(0, CX, step, 0)
 
-    for i in range(3):
-        loads[i].wait()
-    each_plane(lambda x: prep(x, st1))
-    loads[3].wait()
-    well_sums(0)
-    pl.semaphore_wait(barrier, NGX - 1 + NGY - 1)
-    send_one(0)
-
-    eye = jnp.where(
-        lax.broadcasted_iota(jnp.int32, (8, 8), 0) == lax.broadcasted_iota(jnp.int32, (8, 8), 1), 1.0, 0.0
-    )
+    def wells_data():
+        eye = jnp.where(
+            lax.broadcasted_iota(jnp.int32, (8, 8), 0) == lax.broadcasted_iota(jnp.int32, (8, 8), 1), 1.0, 0.0
+        )
+        x1[:, 256:384] = exact_dot(exact_dot(eye, drop_ref[...], flip), place)
+        parent = exact_dot(exact_dot(eye, par_ref[...].astype(F32), flip), place)
+        bottom = exact_dot(bot_ref[...].reshape(1, 8), place)
+        x1[:, 384:512] = jnp.where(lax.broadcasted_iota(jnp.int32, (8, 128), 0) == 0, bottom, parent)
+
+    def column_fields(x):
+        here = pl.ds(pl.multiple_of(x * CY, CY), CY)
+        fields = [st1[f, x] - ns[f, x] * base[f, x] for f in range(3)]
+        fields += [ns[f, x] * q[f + 1, x, 0:CY] for f in range(3)]
+        fields.append(q[0, x, 0:CY] * c0[here])
+        for f, field in enumerate(fields):
+            hi, lo = split(field)
+            dh[here, f * 128 : (f + 1) * 128] = hi
+            dl[here, f * 128 : (f + 1) * 128] = lo
+
     place = jnp.where(
         lax.broadcasted_iota(jnp.int32, (8, 128), 0) + gx * 8 == lax.broadcasted_iota(jnp.int32, (8, 128), 1),
         1.0, 0.0,
     )
     flip = (((1,), (1,)), ((), ()))
-    w0[0:8] = exact_dot(exact_dot(eye, drop_ref[...], flip), place)
-    w0[8:16] = exact_dot(exact_dot(eye, par_ref[...].astype(F32), flip), place)
-    w0[8:9] = exact_dot(bot_ref[...], place)
-    w_copies = []
-    for k in range(1, NGX):
-        w_copies.append(pltpu.make_async_remote_copy(
-            w0, wr.at[k - 1], w_send, w_recv,
-            device_id=(lax.rem(gx + k, NGX), gy), device_id_type=MESH,
-        ))
-    for copy in w_copies:
+
+    for i in range(3):
+        loads[i].wait()
+    for load in loads[4:]:
+        load.start()
+    each_plane(lambda x: prep(x, st1, True))
+    loads[4].wait()
+    pl.semaphore_wait(barrier, NGX - 1 + NGY - 1)
+    k_copies = [
+        pltpu.make_async_remote_copy(
+            st1.at[3, x], hk.at[i], k_send.at[i], k_recv.at[i],
+            device_id=(lax.rem(gx + step, NGX), gy), device_id_type=MESH,
+        )
+        for i, (x, step) in enumerate(((CX - 1, 1), (0, NGX - 1)))
+    ]
+    halo_one = halo_copies(0, st1, hx1, hys1, hy1)
+    for copy in halo_one[:2] + k_copies:
         copy.start()
-
-    loads[4].wait()
+    loads[3].wait()
+    seen = jnp.dot(g[...], mlh[...], preferred_element_type=F32) + jnp.dot(
+        g[...], mll[...], preferred_element_type=F32
+    )
+    well_sums(0, seen[:, 0:128], seen[:, 128:256])
+    send_one(0)
+
+    wells_data()
     pack_rows(st1, hys1, 4)
-    halo_one = halo_copies(0, st1, hx1, hys1, hy1, 4)
-    for copy in halo_one:
-        copy.start()
-
     for f in range(4):
         q[f, CX] = jnp.zeros((CY + 8, NZ), F32)
         for x in range(CX):
@@ -340,23 +398,55 @@
     each_row = lax.broadcasted_iota(jnp.int32, (128, PD), 0)
     for j in range(CX):
         s[j * 128 : (j + 1) * 128] = jnp.where(col == each_row + 128 * j, 1.0, 0.0).astype(BF16)
-    c0[...] = dot2(s[...], cf[...])
+    here_t = ct[...]
+    for j in range(3):
+        same[:, j * 128 : (j + 1) * 128] = jnp.where(
+            here_t == col[:, j * 128 : (j + 1) * 128], 1.0, 0.0
+        ).astype(BF16)
+    edge[:, 0:128] = g[:, 0:128]
+    edge[:, 128:256] = g[:, COLS - 128 : COLS]
+    spot = jnp.where(lanes < 8, lanes * 128, (lanes - 8) * 128 + 127)
+    edge[:, 256:384] = jnp.where((here_t == spot) & (lanes < 16), 1.0, 0.0).astype(BF16)
+    eh[256:384] = jnp.zeros((128, 384), BF16)
+    el[256:384] = jnp.zeros((128, 384), BF16)
+    hi, lo = split(cf[...])
+    both = jnp.dot(s[...], jnp.concatenate([hi, lo], axis=1), preferred_element_type=F32)
+    c0[...] = both[:, 0:128] + both[:, 128:256]
+    lax.fori_loop(0, CX, transmissibility, 0)
+    send_two(0)
+    for copy in halo_one[2:]:
+        copy.start()
+
     for i in range(5, 8):
         loads[i].wait()
-    wait_bytes(wr, w_send)
-    send_two(0)
-    lax.fori_loop(0, CX, transmissibility, 0)
     each_plane(lambda x: inner_faces(x, st1))
+    each_plane(column_fields)
+    gq[...] = jnp.dot(g[...], dh[...], preferred_element_type=F32) + jnp.dot(
+        g[...], dl[...], preferred_element_type=F32
+    )
     send_three(0)
-    for copy in halo_one:
+
+    for copy in k_copies + halo_one:
         copy.wait()
     for side, x, there in ((0, 0, gx > 0), (1, CX - 1, gx < NGX - 1)):
-        txb[side] = harmonic(hx1[side, 3], st1[3, x]) * jnp.where(there, 1.0, 0.0)
+        txb[side] = harmonic(hk[side], st1[3, x]) * jnp.where(there, 1.0, 0.0)
     for side, there in ((0, gy > 0), (1, gy < NGY - 1)):
         tyb[side] = harmonic(hy1[side, 3], hys1[1 - side, 3]) * jnp.where(there, 1.0, 0.0)
-    plane_faces(hx1)
-    row_faces(hy1, hys1)
+    plane_faces(hx1, True)
+    row_faces(hy1, hys1, True)
+    gq[:, 0:384] = gq[:, 0:384] + (
+        jnp.dot(edge[...], eh[...], preferred_element_type=F32)
+        + jnp.dot(edge[...], el[...], preferred_element_type=F32)
+    )
     answers(0)
+
+    both = jnp.dot(same[...], vhl[...], preferred_element_type=F32)
+    drive = gq[:, 768:896] - (both[:, 0:128] + both[:, 128:256])
+    p, sw, sg = (gq[:, f * 128 : (f + 1) * 128] - gq[:, (f + 3) * 128 : (f + 4) * 128] * drive for f in range(3))
+    m1, m2, m3, m4 = mobilities(p, sw, sg)
+    well_sums(1, 0.8 * m1 + m2 + 0.15 * m3, total_mobility(sw, sg))
+    send_one(1)
+    spread_answers()
 
     def update(x):
         here = pl.ds(pl.multiple_of(x * CY, CY), CY)
@@ -364,26 +454,25 @@
         for f in range(3):
             first = base[f, x] + q[f + 1, x, 0:CY] * drive
             st2[f, x] = st1[f, x] - ns[f, x] * first
-        prep(x, st2)
+        prep(x, st2, False)
 
     each_plane(update)
-    well_sums(1)
-    send_one(1)
     pack_rows(st2, hys2, 3)
-    halo_two = halo_copies(1, st2, hx2, hys2, hy2, 3)
-    for copy in halo_two:
-        copy.start()
+    halo_two = halo_copies(1, st2, hx2, hys2, hy2)
     for f in range(3):
         fx[f] = jnp.zeros((CY, NZ), F32)
     send_two(1)
+    for copy in halo_two:
+        copy.start()
     each_plane(lambda x: inner_faces(x, st2))
     press = send_three(1)
     press_ref[...] = exact_dot(place, press, flip)
     for copy in halo_two:
         copy.wait()
-    plane_faces(hx2)
-    row_faces(hy2, hys2)
+    plane_faces(hx2, False)
+    row_faces(hy2, hys2, False)
     answers(1)
+    spread_answers()
 
     def finish(x):
         here = pl.ds(pl.multiple_of(x * CY, CY), CY)
@@ -394,8 +483,17 @@
     each_plane(finish)
     for n in range(2):
         wait_bytes(r1.at[n], ph_send.at[n, 0])
-        wait_bytes(r2.at[n], ph_send.at[n, 1])
+        wait_bytes(in_parts[n], ph_send.at[n, 1])
         wait_bytes(r3.at[n, pl.ds(0, 56)], ph_send.at[n, 2])
+
+
+def write_out(held, press, out, press_out, sem):
+    copies = [pltpu.make_async_copy(held.at[f], out.at[f], sem.at[f]) for f in range(3)]
+    copies.append(pltpu.make_async_copy(press, press_out, sem.at[3]))
+    for copy in copies:
+        copy.start()
+    for copy in copies:
+        copy.wait()
 
 
 def shards(
@@ -403,7 +501,7 @@
     perf_column, perf_owner, perf_well, perf_segment, seg_parent, seg_drop, bottom_press,
 ):
     vmem = pl.BlockSpec(memory_space=pltpu.VMEM)
-    hbm = pl.BlockSpec(memory_space=pl.ANY)
+    hbm = pl.BlockSpec(memory_space=pltpu.HBM)
     cells = (CX, CY, NZ)
     dma = pltpu.SemaphoreType.DMA
     scratch = [
@@ -413,12 +511,13 @@
         pltpu.VMEM(cells, F32),
         pltpu.VMEM((3,) + cells, F32),
         pltpu.VMEM((3,) + cells, F32),
-        pltpu.VMEM((2, 4, CY, NZ), F32),
+        pltpu.VMEM((2, 3, CY, NZ), F32),
         pltpu.VMEM((2, 3, CY, NZ), F32),
         pltpu.VMEM((2, 4, CX, NZ), F32),
         pltpu.VMEM((2, 3, CX, NZ), F32),
         pltpu.VMEM((2, 4, CX, NZ), F32),
         pltpu.VMEM((2, 3, CX, NZ), F32),
+        pltpu.VMEM((2, CY, NZ), F32),
         pltpu.VMEM((4, CX + 1, CY + 8, NZ), F32),
         pltpu.VMEM(cells, F32),
         pltpu.VMEM(cells, F32),
@@ -437,33 +536,55 @@
         pltpu.VMEM((PD, 128), F32),
         pltpu.VMEM((COLS, 256), BF16),
         pltpu.VMEM((COLS, 256), BF16),
+        pltpu.VMEM((PD, PD), BF16),
+        pltpu.VMEM((PD, 128), jnp.int32),
+        pltpu.VMEM((PD, 384), BF16),
+        pltpu.VMEM((COLS, 896), BF16),
+        pltpu.VMEM((COLS, 896), BF16),
+        pltpu.VMEM((PD, 896), F32),
+        pltpu.VMEM((384, 384), BF16),
+        pltpu.VMEM((384, 384), BF16),
+        pltpu.VMEM((PD, 256), BF16),
         pltpu.VMEM((2, 64, 256), F32),
         pltpu.VMEM((2, NGY - 1, 8, 256), F32),
-        pltpu.VMEM((2, 8, 256), F32),
-        pltpu.VMEM((2, NGX - 1, 8, 256), F32),
+        pltpu.VMEM((8, 512), F32),
+        pltpu.VMEM((NGX - 1, 8, 512), F32),
+        pltpu.VMEM((8, 256), F32),
+        pltpu.VMEM((NGX - 1, 8, 256), F32),
         pltpu.VMEM((2, 8, 256), F32),
         pltpu.VMEM((2, 64, 256), F32),
-        pltpu.VMEM((16, 128), F32),
-        pltpu.VMEM((NGX - 1, 16, 128), F32),
-        dma((8,)), dma((2, 4)), dma((2, 4)), dma((2, 3)), dma((2, 3)), dma, dma,
+        pltpu.VMEM((8, 256), F32),
+        pltpu.VMEM((PD,), jnp.int32),
+        pltpu.VMEM((1, PD), jnp.int32),
+        pltpu.VMEM((PD,), jnp.int32),
+        pltpu.VMEM((PD,), jnp.int32),
+        pltpu.VMEM((8, 8), jnp.int32),
+        pltpu.VMEM((8, 8), F32),
+        pltpu.VMEM((8,), F32),
+        dma((7,)), dma((8,)), dma((2, 4)), dma((2, 4)), dma((2,)), dma((2,)), dma((2, 3)), dma((2, 3)),
     ]
-    return pl.pallas_call(
+    fields = (
+        pressure, water_sat, gas_sat, mass_old, pore_volume, permeability, newton_scale, conn_factor,
+        perf_column, perf_owner.reshape(1, PD), perf_well, perf_segment, seg_parent, seg_drop, bottom_press,
+    )
+    results = pl.pallas_call(
         kernel,
-        out_shape=(
-            jax.ShapeDtypeStruct((3,) + cells, F32),
-            jax.ShapeDtypeStruct((8, 8), F32),
-        ),
-        in_specs=[hbm] * 8 + [vmem] * 7,
+        out_shape=(pltpu.VMEM((3,) + cells, F32), pltpu.VMEM((8, 8), F32)),
+        in_specs=[hbm] * 15,
         out_specs=(vmem, vmem),
         scratch_shapes=scratch,
         compiler_params=pltpu.CompilerParams(
-            collective_id=0, has_side_effects=True, vmem_limit_bytes=48 << 20
+            collective_id=0, has_side_effects=True, vmem_limit_bytes=40 << 20
         ),
-    )(
-        pressure, water_sat, gas_sat, mass_old, pore_volume, permeability, newton_scale, conn_factor,
-        perf_column.reshape(1, PD), perf_owner.reshape(1, PD), perf_well.reshape(1, PD),
-        perf_segment.reshape(1, PD), seg_parent, seg_drop, bottom_press.reshape(1, 8),
-    )
+    )(*[pltpu.with_memory_space_constraint(v, pltpu.HBM) for v in fields])
+    return pl.pallas_call(
+        write_out,
+        out_shape=(jax.ShapeDtypeStruct((3,) + cells, F32), jax.ShapeDtypeStruct((8, 8), F32)),
+        in_specs=[vmem, vmem],
+        out_specs=(hbm, hbm),
+        scratch_shapes=[dma((4,))],
+        compiler_params=pltpu.CompilerParams(vmem_limit_bytes=1 << 20),
+    )(*[pltpu.with_memory_space_constraint(v, pltpu.VMEM) for v in results])
 
 
 def solution(mesh):

time: 57.1 us -> 40.7 us (0.71)
  local copies, waits for them, and re-layouts: 14 us -> 0 us
  Pallas kernels: 41.9 us -> 39.9 us
    unnamed x24 -> x0, local copies, waits for them, and re-layouts: 12 us -> none
    reshape x3 -> x0, local copies, waits for them, and re-layouts: 2.05 us -> none  [the longest x1 0.68 us: shards(): perf_column.reshape(1, PD)]
    pallas_call x1 -> x2, Pallas kernels: 41.9 us -> 39.9 us  [the longest x1 38.8 us: shards(): pl.pallas_call(kernel, out_shape=(pltpu.VMEM((3,) + cells, F32), pltpu.VM...]
where the time goes in v1:
time: 40.7 us; the launch traced here: 40.6 us
  Pallas kernels  39.9 us (98%)
  between operations  0.64 us (2%)
    pallas_call x1, Pallas kernels, shards(): pl.pallas_call(kernel, out_shape=(pltpu.VMEM((3,) + cells, F32), pltpu.VM...  38.8 us
    pallas_call x1, Pallas kernels, shards(): pl.pallas_call(write_out, out_shape=(jax.ShapeDtypeStruct((3,) + cells, F...  1.18 us

profile of v1, /device:TPU:1, one launch (start us, length us, event | category | flops | bytes accessed | tf_op | source)
XLA Modules:
  0.0 40.6 jit_solution(788769127785582588)
XLA Ops:
  0.6 38.8 %shard_map.158 = (f32[3,8,128,128]{3,2,1,0:T(8,128)S(1)}, f32[8,8]{1,0:T(8,128)S(1)}) custom-call(f32[8,128,128]{2,1,0:T(8,128)} %p_h.1, f32[8,128,128]{2,1,0:T(8,128)} %sw_h.1, f32[8,128,128]{2,1,0:T(8,128)} %sg_h.1, f32[3,8,128,128]{3,2,1,0:T(8,128)} %mo_h.1, f32[8,128,128]{2,1,0:T(8,128)} %pv_h.1, f32[8,128,128]{2,1,0:T(8,128)} %k_h.1, ...), custom_call_target="tpu_custom_call" | custom-call | tf_op jit(solution)/shard_map/pallas_call | solution.py:570
  39.4 1.2 %shard_map.159 = (f32[3,8,128,128]{3,2,1,0:T(8,128)}, f32[8,8]{1,0:T(8,128)}) custom-call(f32[3,8,128,128]{3,2,1,0:T(8,128)S(1)} %get-tuple-element.4.held, f32[8,8]{1,0:T(8,128)S(1)} %get-tuple-element.5.press), custom_call_target="tpu_custom_call" | custom-call | tf_op jit(solution)/shard_map/pallas_call | solution.py:580

commit v2 on v1

--- a/solution.py
+++ b/solution.py
@@ -63,13 +63,13 @@
 def kernel(
     p_h, sw_h, sg_h, mo_h, pv_h, k_h, ns_h, cf_h,
     col_h, own_h, well_h, seg_h, par_h, drop_h, bot_h,
-    out_ref, press_ref,
+    base, q, s, vhl, press_ref,
     st1, st2, cf, pv, mo, ns, hx1, hx2, hy1, hy2, hys1, hys2,
-    hk, q, tx, ty, tz, txb, tyb, fx, fy, base, c0, wl,
-    g, s, a_t, r, lm, mlh, mll, same, ct, edge, dh, dl, gq, eh, el, vhl,
-    tb, r1, x1, r2, y1, r4, x3, r3, wd,
+    hk, tx, ty, tz, txb, tyb, fx, fy, c0, wl,
+    g, a_t, r, lm, mlh, mll, same, ct, edge, dh, dl, gq, eh, el,
+    tb, r1, x1, r2, y1, r4, x3, r3, w0, wr, wd,
     col_ref, own_ref, well_ref, seg_ref, par_ref, drop_ref, bot_ref,
-    small_sem, load_sem, halo_send, halo_recv, k_send, k_recv, ph_send, ph_recv,
+    small_sem, load_sem, halo_send, halo_recv, k_send, k_recv, w_send, w_recv, ph_send, ph_recv,
 ):
     gx = lax.axis_index("gx")
     gy = lax.axis_index("gy")
@@ -163,10 +163,7 @@
     def send_two(n):
         wait_bytes(r1.at[n], ph_recv.at[n, 0])
         part = tb[n, pl.ds(pl.multiple_of(gy * 8, 8), 8)] + jnp.sum(r1[n], axis=0)
-        if n == 0:
-            x1[:, 0:256] = part
-        else:
-            y1[...] = part
+        out_parts[n][...] = part
         for k in GX_ORDER:
             to = lax.rem(gx + k, NGX)
             pltpu.make_async_remote_copy(
@@ -177,8 +174,6 @@
     def send_three(n):
         wait_bytes(in_parts[n], ph_recv.at[n, 1])
         sums = out_parts[n][...] + jnp.sum(in_parts[n][...], axis=0)
-        if n == 0:
-            wd[...] = sums[:, 256:512]
         drop = wd[:, 0:128]
         parent = wd[:, 128:256]
         dens = (sums[:, 0:128] + 0.5) / (sums[:, 128:256] + 1.0)
@@ -219,6 +214,16 @@
             for x in range(CX):
                 rows[0, f, x : x + 1] = state[f, x, CY - 1 : CY]
                 rows[1, f, x : x + 1] = state[f, x, 0:1]
+
+    def plane_copies(start, size, sems):
+        return [
+            pltpu.make_async_remote_copy(
+                st1.at[pl.ds(start, size), x], hx1.at[side, pl.ds(start, size)],
+                k_send.at[sems + side], k_recv.at[sems + side],
+                device_id=(lax.rem(gx + step, NGX), gy), device_id_type=MESH,
+            )
+            for side, x, step in ((0, CX - 1, 1), (1, 0, NGX - 1))
+        ]
 
     def halo_copies(n, state, planes, rows_out, rows_in):
         up, down = lax.rem(gx + 1, NGX), lax.rem(gx + NGX - 1, NGX)
@@ -273,8 +278,9 @@
             stored2 = (0.98 + 0.02 * p) * sw
             stored3 = (0.2 + 0.8 * p) * sg + (0.2 * p) * stored1
             vol = pv[x, ys]
-            for f, held in enumerate((stored1, stored2, stored3)):
-                base[f, x, ys] = vol * held - mo[f, x, ys] + acc[f]
+            pull = p * c0[pl.ds(pl.multiple_of(x * CY + y0, YB), YB)]
+            for f, (held, m) in enumerate(((stored1, m1), (stored2, m2), (stored3, m34))):
+                base[f, x, ys] = vol * held - mo[f, x, ys] + acc[f] + m * pull
 
     def put_edge(start, size, f, change):
         hi, lo = split(change)
@@ -337,20 +343,50 @@
             return c
         lax.fori_loop(0, CX, step, 0)
 
-    def wells_data():
-        eye = jnp.where(
-            lax.broadcasted_iota(jnp.int32, (8, 8), 0) == lax.broadcasted_iota(jnp.int32, (8, 8), 1), 1.0, 0.0
-        )
-        x1[:, 256:384] = exact_dot(exact_dot(eye, drop_ref[...], flip), place)
-        parent = exact_dot(exact_dot(eye, par_ref[...].astype(F32), flip), place)
-        bottom = exact_dot(bot_ref[...].reshape(1, 8), place)
-        x1[:, 384:512] = jnp.where(lax.broadcasted_iota(jnp.int32, (8, 128), 0) == 0, bottom, parent)
+    def pack_wells_data():
+        steps = lax.broadcasted_iota(jnp.int32, (8, 8), 0)
+        spots = lax.broadcasted_iota(jnp.int32, (8, 8), 1)
+        bottom = jnp.sum(jnp.where(steps == spots, bot_ref[...].reshape(1, 8), 0.0), axis=1, keepdims=True)
+        parent = jnp.where(spots == 0, bottom, par_ref[...].astype(F32))
+        steps = lax.broadcasted_iota(jnp.int32, (8, 128), 0)
+        spots = lax.broadcasted_iota(jnp.int32, (8, 128), 1)
+        repeat = jnp.where((spots & 7) == steps, 1.0, 0.0)
+        both = exact_dot(jnp.concatenate([drop_ref[...], parent], axis=0), repeat)
+        flat = jnp.where((spots >> 3) == steps, both[0:8], 0.0) + jnp.where((spots >> 3) - 8 == steps, both[8:16], 0.0)
+        w0[...] = jnp.sum(flat, axis=0, keepdims=True)
+        wr[gx, 0:1] = w0[...]
+
+    def send_wells_data():
+        for k in GX_ORDER:
+            pltpu.make_async_remote_copy(
+                w0, wr.at[gx, pl.ds(0, 1)], w_send, w_recv,
+                device_id=(lax.rem(gx + k, NGX), gy), device_id_type=MESH,
+            ).start()
+
+    def place_wells_data():
+        wait_bytes(wr.at[pl.ds(0, NGX - 1), pl.ds(0, 1)], w_recv)
+        rows = jnp.concatenate([wr[i, 0:1] for i in range(NGX)], axis=0)
+        parts = []
+        for i in range(3):
+            part = rows.astype(BF16)
+            parts.append(part.astype(F32))
+            rows = rows - parts[-1]
+        spots = lax.broadcasted_iota(jnp.int32, (128, 2048), 1)
+        wanted = ((spots >> 10) << 6) + ((spots & 7) << 3) + ((spots >> 7) & 7)
+        repeat = jnp.where(lax.broadcasted_iota(jnp.int32, (128, 2048), 0) == wanted, 1.0, 0.0).astype(BF16)
+        spread = jnp.dot(jnp.concatenate(parts, axis=0).astype(BF16), repeat, preferred_element_type=F32)
+        spread = (spread[0:16] + spread[16:32]) + spread[32:48]
+        spots = lax.broadcasted_iota(jnp.int32, (NGX, 2048), 1)
+        mine = ((spots & 127) >> 3) == lax.broadcasted_iota(jnp.int32, (NGX, 2048), 0)
+        spread = jnp.sum(jnp.where(mine, spread, 0.0), axis=0, keepdims=True)
+        for seg in range(8):
+            wd[seg : seg + 1, 0:128] = spread[:, seg * 128 : (seg + 1) * 128]
+            wd[seg : seg + 1, 128:256] = spread[:, (seg + 8) * 128 : (seg + 9) * 128]
 
     def column_fields(x):
         here = pl.ds(pl.multiple_of(x * CY, CY), CY)
         fields = [st1[f, x] - ns[f, x] * base[f, x] for f in range(3)]
         fields += [ns[f, x] * q[f + 1, x, 0:CY] for f in range(3)]
-        fields.append(q[0, x, 0:CY] * c0[here])
         for f, field in enumerate(fields):
             hi, lo = split(field)
             dh[here, f * 128 : (f + 1) * 128] = hi
@@ -362,11 +398,18 @@
     )
     flip = (((1,), (1,)), ((), ()))
 
+    pack_wells_data()
+
     for i in range(3):
         loads[i].wait()
     for load in loads[4:]:
         load.start()
     each_plane(lambda x: prep(x, st1, True))
+    loads[3].wait()
+    seen = jnp.dot(g[...], mlh[...], preferred_element_type=F32) + jnp.dot(
+        g[...], mll[...], preferred_element_type=F32
+    )
+    well_sums(0, seen[:, 0:128], seen[:, 128:256])
     loads[4].wait()
     pl.semaphore_wait(barrier, NGX - 1 + NGY - 1)
     k_copies = [
@@ -376,17 +419,14 @@
         )
         for i, (x, step) in enumerate(((CX - 1, 1), (0, NGX - 1)))
     ]
+    send_wells_data()
     halo_one = halo_copies(0, st1, hx1, hys1, hy1)
-    for copy in halo_one[:2] + k_copies:
+    early = plane_copies(0, 1, 2)
+    late = plane_copies(1, 2, 4)
+    for copy in k_copies + early:
         copy.start()
-    loads[3].wait()
-    seen = jnp.dot(g[...], mlh[...], preferred_element_type=F32) + jnp.dot(
-        g[...], mll[...], preferred_element_type=F32
-    )
-    well_sums(0, seen[:, 0:128], seen[:, 128:256])
     send_one(0)
 
-    wells_data()
     pack_rows(st1, hys1, 4)
     for f in range(4):
         q[f, CX] = jnp.zeros((CY + 8, NZ), F32)
@@ -414,19 +454,20 @@
     c0[...] = both[:, 0:128] + both[:, 128:256]
     lax.fori_loop(0, CX, transmissibility, 0)
     send_two(0)
-    for copy in halo_one[2:]:
+    for copy in halo_one[2:] + late:
         copy.start()
 
     for i in range(5, 8):
         loads[i].wait()
     each_plane(lambda x: inner_faces(x, st1))
     each_plane(column_fields)
+    place_wells_data()
     gq[...] = jnp.dot(g[...], dh[...], preferred_element_type=F32) + jnp.dot(
         g[...], dl[...], preferred_element_type=F32
     )
     send_three(0)
 
-    for copy in k_copies + halo_one:
+    for copy in k_copies + early + late + halo_one[2:]:
         copy.wait()
     for side, x, there in ((0, 0, gx > 0), (1, CX - 1, gx < NGX - 1)):
         txb[side] = harmonic(hk[side], st1[3, x]) * jnp.where(there, 1.0, 0.0)
@@ -441,8 +482,8 @@
     answers(0)
 
     both = jnp.dot(same[...], vhl[...], preferred_element_type=F32)
-    drive = gq[:, 768:896] - (both[:, 0:128] + both[:, 128:256])
-    p, sw, sg = (gq[:, f * 128 : (f + 1) * 128] - gq[:, (f + 3) * 128 : (f + 4) * 128] * drive for f in range(3))
+    level = both[:, 0:128] + both[:, 128:256]
+    p, sw, sg = (gq[:, f * 128 : (f + 1) * 128] + gq[:, (f + 3) * 128 : (f + 4) * 128] * level for f in range(3))
     m1, m2, m3, m4 = mobilities(p, sw, sg)
     well_sums(1, 0.8 * m1 + m2 + 0.15 * m3, total_mobility(sw, sg))
     send_one(1)
@@ -450,9 +491,8 @@
 
     def update(x):
         here = pl.ds(pl.multiple_of(x * CY, CY), CY)
-        drive = q[0, x, 0:CY] * c0[here] - wl[here]
         for f in range(3):
-            first = base[f, x] + q[f + 1, x, 0:CY] * drive
+            first = base[f, x] - q[f + 1, x, 0:CY] * wl[here]
             st2[f, x] = st1[f, x] - ns[f, x] * first
         prep(x, st2, False)
 
@@ -472,26 +512,23 @@
     plane_faces(hx2, False)
     row_faces(hy2, hys2, False)
     answers(1)
-    spread_answers()
-
-    def finish(x):
-        here = pl.ds(pl.multiple_of(x * CY, CY), CY)
-        drive = q[0, x, 0:CY] * c0[here] - wl[here]
-        for f in range(3):
-            out_ref[f, x] = base[f, x] + q[f + 1, x, 0:CY] * drive
-
-    each_plane(finish)
+    wait_bytes(wr.at[pl.ds(0, NGX - 1), pl.ds(0, 1)], w_send)
     for n in range(2):
         wait_bytes(r1.at[n], ph_send.at[n, 0])
         wait_bytes(in_parts[n], ph_send.at[n, 1])
         wait_bytes(r3.at[n, pl.ds(0, 56)], ph_send.at[n, 2])
 
 
-def write_out(held, press, out, press_out, sem):
-    copies = [pltpu.make_async_copy(held.at[f], out.at[f], sem.at[f]) for f in range(3)]
-    copies.append(pltpu.make_async_copy(press, press_out, sem.at[3]))
-    for copy in copies:
-        copy.start()
+def finish(base, q, s, vhl, press, out, press_out, held, sem):
+    copies = [pltpu.make_async_copy(press, press_out, sem.at[CX])]
+    copies[0].start()
+    for x in range(CX):
+        both = jnp.dot(s[x * CY : (x + 1) * CY], vhl[...], preferred_element_type=F32)
+        wl = both[:, 0:128] + both[:, 128:256]
+        for f in range(3):
+            held[f, x] = base[f, x] - q[f + 1, x, 0:CY] * wl
+        copies.append(pltpu.make_async_copy(held.at[:, x], out.at[:, x], sem.at[x]))
+        copies[-1].start()
     for copy in copies:
         copy.wait()
 
@@ -518,7 +555,6 @@
         pltpu.VMEM((2, 4, CX, NZ), F32),
         pltpu.VMEM((2, 3, CX, NZ), F32),
         pltpu.VMEM((2, CY, NZ), F32),
-        pltpu.VMEM((4, CX + 1, CY + 8, NZ), F32),
         pltpu.VMEM(cells, F32),
         pltpu.VMEM(cells, F32),
         pltpu.VMEM(cells, F32),
@@ -526,11 +562,9 @@
         pltpu.VMEM((2, CX, NZ), F32),
         pltpu.VMEM((3, CY, NZ), F32),
         pltpu.VMEM((3, CY + 8, NZ), F32),
-        pltpu.VMEM((3,) + cells, F32),
         pltpu.VMEM((COLS, NZ), F32),
         pltpu.VMEM((COLS, NZ), F32),
         pltpu.VMEM((PD, COLS), BF16),
-        pltpu.VMEM((COLS, PD), BF16),
         pltpu.VMEM((64, PD), BF16),
         pltpu.VMEM((PD, 128), BF16),
         pltpu.VMEM((PD, 128), F32),
@@ -539,20 +573,21 @@
         pltpu.VMEM((PD, PD), BF16),
         pltpu.VMEM((PD, 128), jnp.int32),
         pltpu.VMEM((PD, 384), BF16),
-        pltpu.VMEM((COLS, 896), BF16),
-        pltpu.VMEM((COLS, 896), BF16),
-        pltpu.VMEM((PD, 896), F32),
+        pltpu.VMEM((COLS, 768), BF16),
+        pltpu.VMEM((COLS, 768), BF16),
+        pltpu.VMEM((PD, 768), F32),
         pltpu.VMEM((384, 384), BF16),
         pltpu.VMEM((384, 384), BF16),
-        pltpu.VMEM((PD, 256), BF16),
         pltpu.VMEM((2, 64, 256), F32),
         pltpu.VMEM((2, NGY - 1, 8, 256), F32),
-        pltpu.VMEM((8, 512), F32),
-        pltpu.VMEM((NGX - 1, 8, 512), F32),
+        pltpu.VMEM((8, 256), F32),
+        pltpu.VMEM((NGX - 1, 8, 256), F32),
         pltpu.VMEM((8, 256), F32),
         pltpu.VMEM((NGX - 1, 8, 256), F32),
         pltpu.VMEM((2, 8, 256), F32),
         pltpu.VMEM((2, 64, 256), F32),
+        pltpu.VMEM((1, 128), F32),
+        pltpu.VMEM((NGX, 8, 128), F32),
         pltpu.VMEM((8, 256), F32),
         pltpu.VMEM((PD,), jnp.int32),
         pltpu.VMEM((1, PD), jnp.int32),
@@ -561,7 +596,7 @@
         pltpu.VMEM((8, 8), jnp.int32),
         pltpu.VMEM((8, 8), F32),
         pltpu.VMEM((8,), F32),
-        dma((7,)), dma((8,)), dma((2, 4)), dma((2, 4)), dma((2,)), dma((2,)), dma((2, 3)), dma((2, 3)),
+        dma((7,)), dma((8,)), dma((2, 4)), dma((2, 4)), dma((6,)), dma((6,)), dma, dma, dma((2, 3)), dma((2, 3)),
     ]
     fields = (
         pressure, water_sat, gas_sat, mass_old, pore_volume, permeability, newton_scale, conn_factor,
@@ -569,21 +604,27 @@
     )
     results = pl.pallas_call(
         kernel,
-        out_shape=(pltpu.VMEM((3,) + cells, F32), pltpu.VMEM((8, 8), F32)),
+        out_shape=(
+            pltpu.VMEM((3,) + cells, F32),
+            pltpu.VMEM((4, CX + 1, CY + 8, NZ), F32),
+            pltpu.VMEM((COLS, PD), BF16),
+            pltpu.VMEM((PD, 256), BF16),
+            pltpu.VMEM((8, 8), F32),
+        ),
         in_specs=[hbm] * 15,
-        out_specs=(vmem, vmem),
+        out_specs=(vmem,) * 5,
         scratch_shapes=scratch,
         compiler_params=pltpu.CompilerParams(
             collective_id=0, has_side_effects=True, vmem_limit_bytes=40 << 20
         ),
     )(*[pltpu.with_memory_space_constraint(v, pltpu.HBM) for v in fields])
     return pl.pallas_call(
-        write_out,
+        finish,
         out_shape=(jax.ShapeDtypeStruct((3,) + cells, F32), jax.ShapeDtypeStruct((8, 8), F32)),
-        in_specs=[vmem, vmem],
+        in_specs=[vmem] * 5,
         out_specs=(hbm, hbm),
-        scratch_shapes=[dma((4,))],
-        compiler_params=pltpu.CompilerParams(vmem_limit_bytes=1 << 20),
+        scratch_shapes=[pltpu.VMEM((3,) + cells, F32), dma((CX + 1,))],
+        compiler_params=pltpu.CompilerParams(vmem_limit_bytes=6 << 20),
     )(*[pltpu.with_memory_space_constraint(v, pltpu.VMEM) for v in results])
 
 

time: 40.7 us -> 38.9 us (0.956)
  Pallas kernels: 39.9 us -> 38 us
    pallas_call x1, Pallas kernels: 38.8 us -> 36.5 us  [shards(): pl.pallas_call(kernel, out_shape=(pltpu.VMEM((3,) + cells, F32), pltpu.VM...]
where the time goes in v2:
time: 38.9 us; the launch traced here: 38.6 us
  Pallas kernels  38 us (98%)
  between operations  0.64 us (2%)
    pallas_call x1, Pallas kernels, shards(): pl.pallas_call(kernel, out_shape=(pltpu.VMEM((3,) + cells, F32), pltpu.VM...  36.5 us
    pallas_call x1, Pallas kernels, shards(): pl.pallas_call(finish, out_shape=(jax.ShapeDtypeStruct((3,) + cells, F32)...  1.46 us

profile of v2, /device:TPU:1, one launch (start us, length us, event | category | flops | bytes accessed | tf_op | source)
XLA Modules:
  0.0 38.6 jit_solution(5348201103115524785)
XLA Ops:
  0.6 36.5 %shard_map.158 = (f32[3,8,128,128]{3,2,1,0:T(8,128)S(1)}, f32[4,9,136,128]{3,2,1,0:T(8,128)S(1)}, bf16[1024,384]{1,0:T(8,128)(2,1)S(1)}, bf16[384,256]{1,0:T(8,128)(2,1)S(1)}, f32[8,8]{1,0:T(8,128)S(1)}) custom-call(f32[8,128,128]{2,1,0:T(8,128)} %p_h.1, f32[8,128,128]{2,1,0:T(8,128)} %sw_h.1, f32[8,128,128]{2,1,0:T(8,128)} %sg_h.1, ...), custom_call_target="tpu_custom_call" | custom-call | tf_op jit(solution)/shard_map/pallas_call | solution.py:605
  37.2 1.5 %shard_map.159 = (f32[3,8,128,128]{3,2,1,0:T(8,128)}, f32[8,8]{1,0:T(8,128)}) custom-call(f32[3,8,128,128]{3,2,1,0:T(8,128)S(1)} %get-tuple-element.7.base, f32[4,9,136,128]{3,2,1,0:T(8,128)S(1)} %get-tuple-element.8.q, bf16[1024,384]{1,0:T(8,128)(2,1)S(1)} %get-tuple-element.9.s, bf16[384,256]{1,0:T(8,128)(2,1)S(1)} %get-tuple-element.10.vhl, ...), custom_call_target="tpu_custom_call" | custom-call | tf_op jit(solution)/shard_map/pallas_call | solution.py:621

commit v3 on v2

--- a/solution.py
+++ b/solution.py
@@ -93,7 +93,7 @@
         pltpu.make_async_copy(mo_h, mo, load_sem.at[6]),
         pltpu.make_async_copy(ns_h, ns, load_sem.at[7]),
     ]
-    for load in loads[:4]:
+    for load in loads[:5]:
         load.start()
 
     barrier = pltpu.get_barrier_semaphore()
@@ -337,11 +337,11 @@
         tz[x] = jnp.where(zs == NZ - 1, 0.0, 0.1 * harmonic(k, pltpu.roll(k, NZ - 1, 1)))
         return c
 
-    def each_plane(body):
+    def each_plane(body, first=0, last=CX):
         def step(x, c):
             body(x)
             return c
-        lax.fori_loop(0, CX, step, 0)
+        lax.fori_loop(first, last, step, 0)
 
     def pack_wells_data():
         steps = lax.broadcasted_iota(jnp.int32, (8, 8), 0)
@@ -402,7 +402,7 @@
 
     for i in range(3):
         loads[i].wait()
-    for load in loads[4:]:
+    for load in loads[5:]:
         load.start()
     each_plane(lambda x: prep(x, st1, True))
     loads[3].wait()
@@ -502,9 +502,10 @@
     for f in range(3):
         fx[f] = jnp.zeros((CY, NZ), F32)
     send_two(1)
+    each_plane(lambda x: inner_faces(x, st2), 0, 5)
     for copy in halo_two:
         copy.start()
-    each_plane(lambda x: inner_faces(x, st2))
+    each_plane(lambda x: inner_faces(x, st2), 5, CX)
     press = send_three(1)
     press_ref[...] = exact_dot(place, press, flip)
     for copy in halo_two:
@@ -522,13 +523,15 @@
 def finish(base, q, s, vhl, press, out, press_out, held, sem):
     copies = [pltpu.make_async_copy(press, press_out, sem.at[CX])]
     copies[0].start()
-    for x in range(CX):
-        both = jnp.dot(s[x * CY : (x + 1) * CY], vhl[...], preferred_element_type=F32)
-        wl = both[:, 0:128] + both[:, 128:256]
-        for f in range(3):
-            held[f, x] = base[f, x] - q[f + 1, x, 0:CY] * wl
-        copies.append(pltpu.make_async_copy(held.at[:, x], out.at[:, x], sem.at[x]))
-        copies[-1].start()
+    for start in range(0, CX, 2):
+        both = jnp.dot(s[start * CY : (start + 2) * CY], vhl[...], preferred_element_type=F32)
+        for x in range(start, start + 2):
+            here = slice((x - start) * CY, (x - start + 1) * CY)
+            wl = both[here, 0:128] + both[here, 128:256]
+            for f in range(3):
+                held[f, x] = base[f, x] - q[f + 1, x, 0:CY] * wl
+            copies.append(pltpu.make_async_copy(held.at[:, x], out.at[:, x], sem.at[x]))
+            copies[-1].start()
     for copy in copies:
         copy.wait()
 

time: 38.9 us -> 38.7 us (level)
  no operation moved by 1% of the time
where the time goes in v3:
time: 38.7 us; the launch traced here: 38.6 us
  Pallas kernels  38 us (98%)
  between operations  0.64 us (2%)
    pallas_call x1, Pallas kernels, shards(): pl.pallas_call(kernel, out_shape=(pltpu.VMEM((3,) + cells, F32), pltpu.VM...  36.5 us
    pallas_call x1, Pallas kernels, shards(): pl.pallas_call(finish, out_shape=(jax.ShapeDtypeStruct((3,) + cells, F32)...  1.48 us

profile of v3, /device:TPU:1, one launch (start us, length us, event | category | flops | bytes accessed | tf_op | source)
XLA Modules:
  0.0 38.6 jit_solution(14701889373937976728)
XLA Ops:
  0.6 36.5 %shard_map.158 = (f32[3,8,128,128]{3,2,1,0:T(8,128)S(1)}, f32[4,9,136,128]{3,2,1,0:T(8,128)S(1)}, bf16[1024,384]{1,0:T(8,128)(2,1)S(1)}, bf16[384,256]{1,0:T(8,128)(2,1)S(1)}, f32[8,8]{1,0:T(8,128)S(1)}) custom-call(f32[8,128,128]{2,1,0:T(8,128)} %p_h.1, f32[8,128,128]{2,1,0:T(8,128)} %sw_h.1, f32[8,128,128]{2,1,0:T(8,128)} %sg_h.1, ...), custom_call_target="tpu_custom_call" | custom-call | tf_op jit(solution)/shard_map/pallas_call | solution.py:608
  37.1 1.5 %shard_map.159 = (f32[3,8,128,128]{3,2,1,0:T(8,128)}, f32[8,8]{1,0:T(8,128)}) custom-call(f32[3,8,128,128]{3,2,1,0:T(8,128)S(1)} %get-tuple-element.7.base, f32[4,9,136,128]{3,2,1,0:T(8,128)S(1)} %get-tuple-element.8.q, bf16[1024,384]{1,0:T(8,128)(2,1)S(1)} %get-tuple-element.9.s, bf16[384,256]{1,0:T(8,128)(2,1)S(1)} %get-tuple-element.10.vhl, ...), custom_call_target="tpu_custom_call" | custom-call | tf_op jit(solution)/shard_map/pallas_call | solution.py:624

commit v4 on v3

--- a/solution.py
+++ b/solution.py
@@ -116,7 +116,7 @@
     lanes = lax.broadcasted_iota(jnp.int32, (PD, 128), 1)
     ct[...] = col_t
     lm[...] = jnp.where(lane_t == lanes, 1.0, 0.0)
-    r[...] = jnp.where(row_t == lanes, 1.0, 0.0).astype(BF16)
+    r[...] = jnp.where(row_t == (lanes & 63), 1.0, 0.0).astype(BF16)
     for j in range(CX):
         g[:, j * 128 : (j + 1) * 128] = jnp.where(col_t == lanes + 128 * j, 1.0, 0.0).astype(BF16)
     rows64 = lax.broadcasted_iota(jnp.int32, (64, PD), 0)
@@ -197,7 +197,7 @@
 
     def answers(n):
         wait_bytes(r3.at[n, pl.ds(0, 56)], ph_recv.at[n, 2])
-        seen = dot2(r[:, 0:64], r3[n])
+        seen = jnp.dot(r[...], jnp.concatenate(split(r3[n]), axis=0), preferred_element_type=F32)
         press = jnp.sum(lm[...] * seen[:, 0:128], axis=1, keepdims=True)
         dens = jnp.sum(lm[...] * seen[:, 128:256], axis=1, keepdims=True)
         depth = (lax.broadcasted_iota(jnp.int32, (1, NZ), 1).astype(F32) + 0.5) / NZ - 0.5

time: 38.7 us -> 38.6 us (level)
  no operation moved by 1% of the time
where the time goes in v4:
time: 38.6 us; the launch traced here: 38.4 us
  Pallas kernels  37.8 us (98%)
  between operations  0.64 us (2%)
    pallas_call x1, Pallas kernels, shards(): pl.pallas_call(kernel, out_shape=(pltpu.VMEM((3,) + cells, F32), pltpu.VM...  36.3 us
    pallas_call x1, Pallas kernels, shards(): pl.pallas_call(finish, out_shape=(jax.ShapeDtypeStruct((3,) + cells, F32)...  1.48 us

profile of v4, /device:TPU:1, one launch (start us, length us, event | category | flops | bytes accessed | tf_op | source)
XLA Modules:
  0.0 38.4 jit_solution(5881652897260147197)
XLA Ops:
  0.6 36.3 %shard_map.158 = (f32[3,8,128,128]{3,2,1,0:T(8,128)S(1)}, f32[4,9,136,128]{3,2,1,0:T(8,128)S(1)}, bf16[1024,384]{1,0:T(8,128)(2,1)S(1)}, bf16[384,256]{1,0:T(8,128)(2,1)S(1)}, f32[8,8]{1,0:T(8,128)S(1)}) custom-call(f32[8,128,128]{2,1,0:T(8,128)} %p_h.1, f32[8,128,128]{2,1,0:T(8,128)} %sw_h.1, f32[8,128,128]{2,1,0:T(8,128)} %sg_h.1, ...), custom_call_target="tpu_custom_call" | custom-call | tf_op jit(solution)/shard_map/pallas_call | solution.py:608
  36.9 1.5 %shard_map.159 = (f32[3,8,128,128]{3,2,1,0:T(8,128)}, f32[8,8]{1,0:T(8,128)}) custom-call(f32[3,8,128,128]{3,2,1,0:T(8,128)S(1)} %get-tuple-element.7.base, f32[4,9,136,128]{3,2,1,0:T(8,128)S(1)} %get-tuple-element.8.q, bf16[1024,384]{1,0:T(8,128)(2,1)S(1)} %get-tuple-element.9.s, bf16[384,256]{1,0:T(8,128)(2,1)S(1)} %get-tuple-element.10.vhl, ...), custom_call_target="tpu_custom_call" | custom-call | tf_op jit(solution)/shard_map/pallas_call | solution.py:624
